TPU v7x, 32 devices: a whole 2x2x4 slice. The times are simulated.
32 devices in a mesh: space: 4 (over z), chaos: 8 (over y, x, core).
Axes of the slice: x: 2, y: 2, z: 4, core: 2. Of those that a mesh axis runs over, the one named last changes fastest.
Arguments:
- forcing: float32 [912, 16, 128], P('chaos', 'space'), may hold values from -120 to 120
- mean_field: float32 [16, 128], P('space'), may hold values from 1 to 8
- modes: float32 [12, 16, 128], P(None, 'space'), may hold values from 0.02 to 0.05
- lengths: int32 [8], replicated, may hold values from 1 to 114, 455 in all
Outputs:
- solution: float32 [912, 16, 128], P('chaos', 'space')
- norms: float32 [3], replicated
Inputs may be any that keep to these rules, and one draw needn't show every extreme that they name: Group lengths are positive, sum to 455, and the largest is exactly 114.
All inputs are finite; a program needn't handle non-finite values.
Results may differ from a plain program's by a relative error of at most 0.0001.
Values sent between devices are 32-bit elements; how exact they have to be, the bound alone decides.
A program may use at most 64 MiB of HBM per device.

v0:
```python
import functools
import math

import jax
import jax.numpy as jnp
import numpy as np
from jax import lax
from jax.experimental import pallas as pl
from jax.experimental.pallas import tpu as pltpu
from jax.sharding import PartitionSpec as P

M = 12
P_SIZE = 455
ITERS = 3
LOW = 91
LP = 96
HP = 368
NP = LP + HP
HALO = 3
SIDE = 4

spectrum_low = 0.05
spectrum_high = 3.0
F32 = jnp.float32
BF16 = jnp.bfloat16


def place(p):
    return p if p < LOW else p + (LP - LOW)


def tables():
    indices = [()]
    indices += [(a,) for a in range(M)]
    indices += [(a, b) for a in range(M) for b in range(a, M)]
    indices += [(a, b, c) for a in range(M) for b in range(a, M) for c in range(b, M)]
    lookup = {entry: number for number, entry in enumerate(indices)}
    to_low = np.zeros((M * LP, NP), np.float32)
    to_high = np.zeros((HP, M * LP), np.float32)
    scale = np.ones((NP,), np.float64)
    for number, entry in enumerate(indices):
        scale[place(number)] = math.sqrt(math.prod(math.factorial(entry.count(k)) for k in set(entry)))
        if len(entry) == 3:
            continue
        for k in range(M):
            other = lookup[tuple(sorted(entry + (k,)))]
            to_low[k * LP + number, place(other)] = entry.count(k) + 1
            if other < LOW:
                to_low[k * LP + other, place(number)] = 1.0
            else:
                to_high[place(other) - LP, k * LP + number] = 1.0
    scales = np.stack([1.0 / scale, scale]).astype(np.float32)
    scales = np.ascontiguousarray(np.broadcast_to(scales[:, :, None], (2, NP, 128)))
    return to_low, to_high, scales


def round_up(value, unit):
    return -(-value // unit) * unit


def halves(x):
    hi = x.astype(BF16)
    return hi, (x - hi.astype(F32)).astype(BF16)


def kernel(groups, tiles, cap, rows, cols, lengths_ref, forcing_ref, mean_ref, modes_ref, low_hbm, high_hbm, scale_ref,
           out_ref, norms_ref,
           low_ref, high_ref, send_ref, recv_ref, own_ref, up_ref, down_ref, field_ref, coef_ref, dinv_ref,
           hot_ref, d_ref, r_ref, s_ref, db_ref, v_ref, wb_ref, rsend_ref, rrecv_ref, part_ref, nbuf_ref, zpart_ref, zbuf_ref,
           load_sem, f_send, f_recv, h_send, h_recv, a_send, a_recv, b_send, b_recv, n_send, n_recv, z_send, z_recv):
    me = lax.axis_index("chaos")
    sp = lax.axis_index("space")
    width = cols // groups
    stride = width + 2 * SIDE
    lanes = d_ref.shape[1]
    capp = recv_ref.shape[1]
    half = rsend_ref.shape[1]
    nx = rows * tiles
    total_rows = rows + 2 * HALO
    mesh_id = pl.DeviceIdType.MESH

    load_low = pltpu.make_async_copy(low_hbm, low_ref, load_sem.at[0])
    load_high = pltpu.make_async_copy(high_hbm, high_ref, load_sem.at[1])
    load_low.start()
    load_high.start()

    barrier = pltpu.get_barrier_semaphore()

    def greet_group(j, carry):
        pl.semaphore_signal(barrier, inc=1, device_id=(sp, lax.rem(me + j, groups)), device_id_type=mesh_id)
        return carry

    def greet_column(j, carry):
        pl.semaphore_signal(barrier, inc=1, device_id=(lax.rem(sp + j, tiles), me), device_id_type=mesh_id)
        return carry

    lax.fori_loop(1, groups, greet_group, 0)
    lax.fori_loop(1, tiles, greet_column, 0)

    lane128 = lax.broadcasted_iota(jnp.int32, (cap, 128), 1)

    def pack(j, carry):
        c = lax.rem(me + j, groups)
        base = c * width - SIDE
        block = jnp.zeros((cap, 128), F32)
        for r in range(rows):
            shift = lax.rem(r * stride - base + 256, 128)
            rolled = pltpu.roll(forcing_ref[:, r, :], shift, 1)
            block = jnp.where((lane128 >= r * stride) & (lane128 < (r + 1) * stride), rolled, block)
        send_ref[j, 0:cap, :] = block
        if capp > cap:
            send_ref[j, cap:capp, :] = jnp.zeros((capp - cap, 128), F32)
        return carry

    lax.fori_loop(0, groups, pack, 0)
    field_ref[1, 0] = mean_ref[...]
    field_ref[1, 1:] = modes_ref[...]

    pl.semaphore_wait(barrier, groups - 1 + tiles - 1)

    def a2a(j):
        c = lax.rem(me + j, groups)
        return pltpu.make_async_remote_copy(
            src_ref=send_ref.at[j], dst_ref=recv_ref.at[me], send_sem=a_send.at[j], recv_sem=a_recv.at[me],
            device_id=(sp, c), device_id_type=mesh_id)

    def a2a_in(j):
        c = lax.rem(me + j, groups)
        return pltpu.make_async_remote_copy(
            src_ref=send_ref.at[j], dst_ref=recv_ref.at[c], send_sem=a_send.at[j], recv_sem=a_recv.at[c],
            device_id=(sp, c), device_id_type=mesh_id)

    def start_a2a(j, carry):
        a2a(j).start()
        return carry

    lax.fori_loop(1, groups, start_a2a, 0)

    def column(src, dst, send, recv, target):
        return pltpu.make_async_remote_copy(
            src_ref=src, dst_ref=dst, send_sem=send, recv_sem=recv, device_id=(target, me), device_id_type=mesh_id)

    up_target = lax.rem(sp + tiles - 1, tiles)
    down_target = lax.rem(sp + 1, tiles)
    has_up = sp > 0
    has_down = sp < tiles - 1
    f_up = column(field_ref.at[1], field_ref.at[2], f_send.at[0], f_recv.at[1], up_target)
    f_down = column(field_ref.at[1], field_ref.at[0], f_send.at[1], f_recv.at[0], down_target)
    f_from_up = column(field_ref.at[1], field_ref.at[0], f_send.at[0], f_recv.at[0], up_target)
    f_from_down = column(field_ref.at[1], field_ref.at[2], f_send.at[1], f_recv.at[1], down_target)

    @pl.when(has_up)
    def _():
        f_up.start()

    @pl.when(has_down)
    def _():
        f_down.start()

    recv_ref[me] = send_ref[0]

    slots = groups * capp
    slot = lax.broadcasted_iota(jnp.int32, (1, slots), 1)
    coef = jnp.full((1, slots), -1, jnp.int32)
    start = jnp.int32(0)
    starts = []
    for g in range(groups):
        count = lengths_ref[g]
        here = slot - g * capp
        coef = jnp.where((here >= 0) & (here < count), start + here, coef)
        starts.append(start)
        start = start + count
    row = lax.broadcasted_iota(jnp.int32, (NP, slots), 0)
    row_coef = jnp.where(row < LOW, row, jnp.where(row < LP, -2, row - (LP - LOW)))
    hot_ref[...] = jnp.where(row_coef == coef, 1.0, 0.0).astype(BF16)

    @pl.when(jnp.logical_not(has_up))
    def _():
        field_ref[0] = jnp.zeros(field_ref.shape[1:], F32)
        up_ref[...] = jnp.zeros(up_ref.shape, F32)

    @pl.when(jnp.logical_not(has_down))
    def _():
        field_ref[2] = jnp.zeros(field_ref.shape[1:], F32)
        down_ref[...] = jnp.zeros(down_ref.shape, F32)

    @pl.when(has_up)
    def _():
        f_up.wait_send()
        f_from_up.wait_recv()

    @pl.when(has_down)
    def _():
        f_down.wait_send()
        f_from_down.wait_recv()

    base = me * width - SIDE
    n_fields = M + 1
    lane_f = lax.broadcasted_iota(jnp.int32, (n_fields, lanes), 1)
    col_f = lax.broadcasted_iota(jnp.int32, (n_fields, cols), 1)
    first_field = lax.broadcasted_iota(jnp.int32, (n_fields, cols), 0) == 0

    def field_row(g):
        x = field_ref[g // rows, :, g % rows, :]
        return jnp.where(first_field, x, x * x[0:1, :])

    skip = rows - HALO - 1
    fields = [field_row(skip + g) for g in range(total_rows + 2)]
    packed = [jnp.zeros((n_fields, lanes), F32) for _ in range(4)]
    valid = jnp.zeros((1, lanes), jnp.bool_)
    lane1 = lax.broadcasted_iota(jnp.int32, (1, lanes), 1)
    for r in range(total_rows):
        here = fields[r + 1]
        east = jnp.where(col_f < cols - 1, pltpu.roll(here, cols - 1, 1), 0.0)
        west = jnp.where(col_f > 0, pltpu.roll(here, 1, 1), 0.0)
        shift = lax.rem(r * stride - base + 512, 128)
        at = lane1 - r * stride
        inside = ((at >= 0) & (at < stride) & (at + base >= 0) & (at + base < cols)
                  & (sp * rows - HALO + r >= 0) & (sp * rows - HALO + r < nx))
        valid = valid | inside
        for n, other in enumerate((east, west, fields[r + 2], fields[r])):
            rolled = pltpu.roll(0.5 * (here + other), shift, 1)
            if lanes > 128:
                rolled = jnp.concatenate([rolled] * (lanes // 128), axis=1)
            packed[n] = jnp.where(inside, rolled, packed[n])
    for n in range(4):
        coef_ref[n] = packed[n]
    diagonal = packed[0][0:1] + packed[1][0:1] + packed[2][0:1] + packed[3][0:1]
    dinv_ref[...] = jnp.where(valid, 1.0 / jnp.where(valid, diagonal, 1.0), 0.0)

    def wait_a2a(j, carry):
        a2a(j).wait_send()
        a2a_in(j).wait_recv()
        return carry

    lax.fori_loop(1, groups, wait_a2a, 0)
    hi, lo = halves(recv_ref[...].reshape(slots, 128))
    both = jnp.dot(hot_ref[...], jnp.concatenate([hi, lo], axis=1), preferred_element_type=F32)
    own_ref[...] = (both[:, :128] + both[:, 128:]) * scale_ref[0]

    h_up = column(own_ref, down_ref, h_send.at[0], h_recv.at[1], up_target)
    h_down = column(own_ref, up_ref, h_send.at[1], h_recv.at[0], down_target)
    h_from_up = column(own_ref, up_ref, h_send.at[0], h_recv.at[0], up_target)
    h_from_down = column(own_ref, down_ref, h_send.at[1], h_recv.at[1], down_target)

    @pl.when(has_up)
    def _():
        h_up.start()

    @pl.when(has_down)
    def _():
        h_down.start()

    @pl.when(has_up)
    def _():
        h_up.wait_send()
        h_from_up.wait_recv()

    @pl.when(has_down)
    def _():
        h_down.wait_send()
        h_from_down.wait_recv()

    lane_n = lax.broadcasted_iota(jnp.int32, (NP, 128), 1)

    def spread(block, lower, upper, shift):
        block = jnp.where((lane_n >= lower) & (lane_n < upper), block, 0.0)
        if lanes > 128:
            block = jnp.concatenate([block, jnp.zeros((NP, lanes - 128), F32)], axis=1)
        return pltpu.roll(block, shift % lanes, 1)

    above = (rows - HALO) * stride
    r0 = spread(own_ref[...], 0, rows * stride, HALO * stride)
    r0 = r0 + spread(up_ref[...], above, rows * stride, -above)
    r0 = r0 + spread(down_ref[...], 0, HALO * stride, (HALO + rows) * stride)
    r_ref[...] = r0

    theta = (spectrum_high + spectrum_low) / 2.0
    delta = (spectrum_high - spectrum_low) / 2.0
    sigma = theta / delta
    rho = 1.0 / sigma
    d_ref[...] = r0 * (dinv_ref[...] * (1.0 / theta))
    s_ref[...] = d_ref[...]

    own_lane = jnp.zeros((1, lanes), jnp.bool_)
    for r in range(rows):
        at = lane1 - (HALO + r) * stride - SIDE
        own_lane = own_lane | ((at >= 0) & (at < width))
    own_f = jnp.where(own_lane, 1.0, 0.0)

    load_low.wait()
    load_high.wait()
    part_ref[...] = jnp.zeros(part_ref.shape, F32)

    def neighbours(x):
        return (pltpu.roll(x, lanes - 1, 1), pltpu.roll(x, 1, 1),
                pltpu.roll(x, lanes - stride, 1), pltpu.roll(x, stride, 1))

    CH = 16

    def split_rows(i, carry):
        at = pl.multiple_of(i * CH, CH)
        hi, lo = halves(d_ref[pl.ds(at, CH), :])
        db_ref[pl.ds(at, CH), 0:lanes] = hi
        db_ref[pl.ds(at, CH), lanes:] = lo
        return carry

    def low_terms(i, carry):
        at = pl.multiple_of(i * CH, CH)
        x = d_ref[pl.ds(at, CH), :]
        diffs = [x - y for y in neighbours(x)]
        for k in range(M):
            w = coef_ref[0, k + 1:k + 2, :] * diffs[0]
            for n in range(1, 4):
                w = w + coef_ref[n, k + 1:k + 2, :] * diffs[n]
            hi, lo = halves(w)
            there = pl.multiple_of(k * LP + at, CH)
            wb_ref[pl.ds(there, CH), 0:lanes] = hi
            wb_ref[pl.ds(there, CH), lanes:] = lo
        return carry

    def low_result(i, carry):
        at = pl.multiple_of(i * CH, CH)
        x = d_ref[pl.ds(at, CH), :]
        sums = [coef_ref[n, 0:1, :] * x for n in range(4)]
        for k in range(M):
            there = pl.multiple_of(k * LP + at, CH)
            v = v_ref[pl.ds(there, CH), 0:lanes] + v_ref[pl.ds(there, CH), lanes:]
            for n in range(4):
                sums[n] = sums[n] + coef_ref[n, k + 1:k + 2, :] * v
        result = (sums[0] + sums[1]) + (sums[2] + sums[3])
        result = result - pltpu.roll(sums[0], 1, 1) - pltpu.roll(sums[1], lanes - 1, 1)
        result = result - pltpu.roll(sums[2], stride, 1) - pltpu.roll(sums[3], lanes - stride, 1)
        r_ref[pl.ds(at, CH), :] = r_ref[pl.ds(at, CH), :] - result
        return carry

    def high_result(i, carry):
        at = pl.multiple_of(i * CH, CH)
        x = d_ref[pl.ds(LP + at, CH), :]
        result = v_ref[pl.ds(at, CH), 0:lanes] + v_ref[pl.ds(at, CH), lanes:]
        for n, y in enumerate(neighbours(x)):
            result = result + coef_ref[n, 0:1, :] * (x - y)
        r_ref[pl.ds(LP + at, CH), :] = r_ref[pl.ds(LP + at, CH), :] - result
        return carry

    def back(j):
        c = lax.rem(me + j, groups)
        return pltpu.make_async_remote_copy(
            src_ref=rsend_ref.at[c], dst_ref=rrecv_ref.at[me], send_sem=b_send.at[j], recv_sem=b_recv.at[me],
            device_id=(sp, c), device_id_type=mesh_id)

    def back_in(j):
        c = lax.rem(me + j, groups)
        return pltpu.make_async_remote_copy(
            src_ref=rsend_ref.at[c], dst_ref=rrecv_ref.at[c], send_sem=b_send.at[j], recv_sem=b_recv.at[c],
            device_id=(sp, c), device_id_type=mesh_id)

    def send_back():
        piece = rows * width
        s = s_ref[...]
        q1 = jnp.zeros((NP, 128), F32)
        q2 = jnp.zeros((NP, 128), F32)
        for r in range(rows):
            origin = (HALO + r) * stride + SIDE
            a = pltpu.roll(s, (r * width - origin) % lanes, 1)[:, :128]
            b = pltpu.roll(s, (piece + r * width - origin) % lanes, 1)[:, :128]
            q1 = jnp.where((lane_n >= r * width) & (lane_n < (r + 1) * width), a, q1)
            q2 = jnp.where((lane_n >= piece + r * width) & (lane_n < piece + (r + 1) * width), b, q2)
        p_lane = lax.broadcasted_iota(jnp.int32, (half, NP), 1)
        p_coef = jnp.where(p_lane < LOW, p_lane, jnp.where(p_lane < LP, -2, p_lane - (LP - LOW)))
        t = lax.broadcasted_iota(jnp.int32, (half, NP), 0)
        operands = []
        for q in (q1, q2):
            hi, lo = halves(q * scale_ref[1])
            operands.append(jnp.concatenate([hi, lo], axis=1))
        for g in range(groups):
            block = None
            for h in range(2):
                tt = t + h * half
                hot = jnp.where((tt < lengths_ref[g]) & (p_coef == starts[g] + tt), 1.0, 0.0).astype(BF16)
                term = jnp.dot(hot, operands[h], preferred_element_type=F32)
                block = term if block is None else block + term
            rsend_ref[g] = block[:, :128] + block[:, 128:]

        def start_back(j, carry):
            back(j).start()
            return carry

        lax.fori_loop(1, groups, start_back, 0)
        rrecv_ref[me] = rsend_ref[me]

    weight = scale_ref[1] * scale_ref[1]
    if lanes > 128:
        weight = jnp.concatenate([weight] * (lanes // 128), axis=1)
    for step in range(ITERS):
        lax.fori_loop(0, NP // CH, split_rows, 0)
        lax.fori_loop(0, LP // CH, low_terms, 0)
        v_ref[...] = jnp.dot(low_ref[...], db_ref[...], preferred_element_type=F32)
        lax.fori_loop(0, LP // CH, low_result, 0)
        v_ref[0:HP, :] = jnp.dot(high_ref[...], wb_ref[...], preferred_element_type=F32)
        lax.fori_loop(0, HP // CH, high_result, 0)
        res = r_ref[...]
        part = jnp.sum(res * res * weight, axis=0, keepdims=True) * own_f
        folded = part[:, 0:128]
        for extra in range(1, lanes // 128):
            folded = folded + part[:, extra * 128:(extra + 1) * 128]
        part_ref[step:step + 1, :] = folded
        if step + 1 < ITERS:
            rho_new = 1.0 / (2.0 * sigma - rho)
            new = (rho_new * rho) * d_ref[...] + (2.0 * rho_new / delta) * (res * dinv_ref[...])
            d_ref[...] = new
            s_ref[...] = s_ref[...] + new
            rho = rho_new
            if step + 2 == ITERS:
                send_back()

    def norm_copy(j, slot):
        c = lax.rem(me + j, groups)
        return pltpu.make_async_remote_copy(
            src_ref=part_ref, dst_ref=nbuf_ref.at[c if slot else me], send_sem=n_send.at[j],
            recv_sem=n_recv.at[c if slot else me], device_id=(sp, c), device_id_type=mesh_id)

    def z_copy(j, slot):
        z = lax.rem(sp + j, tiles)
        return pltpu.make_async_remote_copy(
            src_ref=zpart_ref, dst_ref=zbuf_ref.at[z if slot else sp], send_sem=z_send.at[j],
            recv_sem=z_recv.at[z if slot else sp], device_id=(z, me), device_id_type=mesh_id)

    def n_start(j, carry):
        norm_copy(j, False).start()
        return carry

    def n_wait(j, carry):
        norm_copy(j, False).wait_send()
        norm_copy(j, True).wait_recv()
        return carry

    def z_start(j, carry):
        z_copy(j, False).start()
        return carry

    def z_wait(j, carry):
        z_copy(j, False).wait_send()
        z_copy(j, True).wait_recv()
        return carry

    def back_wait(j, carry):
        back(j).wait_send()
        back_in(j).wait_recv()
        return carry

    lax.fori_loop(1, groups, n_start, 0)
    nbuf_ref[me] = part_ref[...]
    lax.fori_loop(1, groups, n_wait, 0)
    zpart_ref[...] = jnp.sum(nbuf_ref[...], axis=0)
    lax.fori_loop(1, tiles, z_start, 0)
    zbuf_ref[sp] = zpart_ref[...]

    lax.fori_loop(1, groups, back_wait, 0)
    piece = rows * width
    lane_h = lax.broadcasted_iota(jnp.int32, (half, 128), 1)
    for h in range(2):
        count = min(half, cap - h * half)
        for r in range(rows):
            block = jnp.zeros((half, 128), F32)
            for c in range(groups):
                rolled = pltpu.roll(rrecv_ref[c], (c * width - h * piece - r * width) % 128, 1)
                block = jnp.where((lane_h >= c * width) & (lane_h < (c + 1) * width), rolled, block)
            out_ref[h * half:h * half + count, r, :] = block[0:count]

    lax.fori_loop(1, tiles, z_wait, 0)
    total = jnp.sum(jnp.sum(zbuf_ref[...], axis=0), axis=1, keepdims=True)
    norms_ref[...] = jnp.broadcast_to(jnp.sqrt(total), norms_ref.shape)


def local(groups, tiles, forcing, mean_field, modes, lengths):
    cap, rows, cols = forcing.shape
    width = cols // groups
    stride = width + 2 * SIDE
    lanes = round_up((rows + 2 * HALO) * stride, 128)
    capp = round_up(cap, 8)
    half = round_up(-(-cap // 2), 16)
    low, high, scales = tables()
    vmem = pl.BlockSpec(memory_space=pltpu.VMEM)
    hbm = pl.BlockSpec(memory_space=pl.ANY)
    dma = pltpu.SemaphoreType.DMA
    out, norms = pl.pallas_call(
        functools.partial(kernel, groups, tiles, cap, rows, cols),
        out_shape=(jax.ShapeDtypeStruct((cap, rows, cols), F32), jax.ShapeDtypeStruct((8, 128), F32)),
        in_specs=[pl.BlockSpec(memory_space=pltpu.SMEM), vmem, vmem, vmem, hbm, hbm, vmem],
        out_specs=(vmem, vmem),
        scratch_shapes=[
            pltpu.VMEM((M * LP, NP), BF16), pltpu.VMEM((HP, M * LP), BF16),
            pltpu.VMEM((groups, capp, 128), F32), pltpu.VMEM((groups, capp, 128), F32),
            pltpu.VMEM((NP, 128), F32), pltpu.VMEM((NP, 128), F32), pltpu.VMEM((NP, 128), F32),
            pltpu.VMEM((3, M + 1, rows, cols), F32), pltpu.VMEM((4, M + 1, lanes), F32), pltpu.VMEM((1, lanes), F32),
            pltpu.VMEM((NP, groups * capp), BF16),
            pltpu.VMEM((NP, lanes), F32), pltpu.VMEM((NP, lanes), F32), pltpu.VMEM((NP, lanes), F32),
            pltpu.VMEM((NP, 2 * lanes), BF16), pltpu.VMEM((M * LP, 2 * lanes), F32), pltpu.VMEM((M * LP, 2 * lanes), BF16),
            pltpu.VMEM((groups, half, 128), F32), pltpu.VMEM((groups, half, 128), F32),
            pltpu.VMEM((8, 128), F32), pltpu.VMEM((groups, 8, 128), F32),
            pltpu.VMEM((8, 128), F32), pltpu.VMEM((tiles, 8, 128), F32),
            dma((2,)), dma((2,)), dma((2,)), dma((2,)), dma((2,)),
            dma((groups,)), dma((groups,)), dma((groups,)), dma((groups,)),
            dma((groups,)), dma((groups,)), dma((tiles,)), dma((tiles,)),
        ],
        compiler_params=pltpu.CompilerParams(collective_id=0, has_side_effects=True, vmem_limit_bytes=48 * 2**20),
        name="chebyshev",
    )(lengths, forcing, mean_field, modes, jnp.asarray(low, BF16), jnp.asarray(high, BF16), jnp.asarray(scales))
    return out, norms[:ITERS, 0]


def solution(mesh):
    in_specs = (P("chaos", "space", None), P("space", None), P(None, "space", None), P())
    out_specs = (P("chaos", "space", None), P())
    body = functools.partial(local, mesh.shape["chaos"], mesh.shape["space"])
    return jax.shard_map(body, mesh=mesh, in_specs=in_specs, out_specs=out_specs, check_vma=False)
```

profile of v0, /device:TPU:0, one launch (start us, length us, event | category | flops | bytes accessed | tf_op | source)
XLA Modules:
  0.0 56.7 jit_solution(852298761508784813)
XLA Ops:
  0.6 0.0 copy-start
  0.6 1.3 %copy-done = bf16[1152,464]{1,0:T(8,128)(2,1)S(1)} copy-done((bf16[1152,464]{1,0:T(8,128)(2,1)S(1)}, bf16[1152,464]{1,0:T(8,128)(2,1)}, u32[]{:S(2)}) %copy-start) | copy-done | bytes 1069080
  1.9 0.0 copy-start.1
  1.9 1.2 %copy-done.1 = bf16[368,1152]{1,0:T(8,128)(2,1)S(1)} copy-done((bf16[368,1152]{1,0:T(8,128)(2,1)S(1)}, bf16[368,1152]{1,0:T(8,128)(2,1)}, u32[]{:S(2)}) %copy-start.1) | copy-done | bytes 847896
  3.1 0.0 copy-start.2
  3.1 1.0 %copy-done.2 = f32[2,464,128]{2,1,0:T(8,128)S(1)} copy-done((f32[2,464,128]{2,1,0:T(8,128)S(1)}, f32[2,464,128]{2,1,0:T(8,128)}, u32[]{:S(2)}) %copy-start.2) | copy-done | bytes 475160
  4.1 0.0 copy-start.3
  4.1 0.9 %copy-done.3 = f32[114,4,128]{2,1,0:T(4,128)S(1)} copy-done((f32[114,4,128]{2,1,0:T(4,128)S(1)}, f32[114,4,128]{2,1,0:T(4,128)}, u32[]{:S(2)}) %copy-start.3) | copy-done | bytes 233496
  5.0 0.0 copy-start.4
  5.0 0.7 %copy-done.4 = f32[12,4,128]{2,1,0:T(4,128)S(1)} copy-done((f32[12,4,128]{2,1,0:T(4,128)S(1)}, f32[12,4,128]{2,1,0:T(4,128)}, u32[]{:S(2)}) %copy-start.4) | copy-done | bytes 24600
  5.8 0.0 copy-start.5
  5.8 0.7 %copy-done.5 = f32[4,128]{1,0:T(4,128)S(1)} copy-done((f32[4,128]{1,0:T(4,128)S(1)}, f32[4,128]{1,0:T(4,128)}, u32[]{:S(2)}) %copy-start.5) | copy-done | bytes 2072
  6.4 0.0 copy-start.6
  6.4 0.7 %copy-done.6 = s32[8]{0:T(128)S(1)} copy-done((s32[8]{0:T(128)S(1)}, s32[8]{0:T(128)}, u32[]{:S(2)}) %copy-start.6) | copy-done | bytes 56
  7.1 48.3 %chebyshev.1 = (f32[114,4,128]{2,1,0:T(4,128)S(1)}, f32[8,128]{1,0:T(8,128)S(1)}) custom-call(s32[8]{0:T(128)S(1)} %copy-done.6, f32[114,4,128]{2,1,0:T(4,128)S(1)} %copy-done.3, f32[4,128]{1,0:T(4,128)S(1)} %copy-done.5, f32[12,4,128]{2,1,0:T(4,128)S(1)} %copy-done.4, bf16[1152,464]{1,0:T(8,128)(2,1)S(1)} %copy-done, bf16[368,1152]{1,0:T(8,128)(2,1)S(1)} %copy-done.1, ...), custom_call_target="tpu_custom_call" | custom-call | tf_op jit(solution)/shard_map/chebyshev/pallas_call | solution.py:487
  55.4 0.6 %slice_reduce_fusion = f32[3]{0:T(128)} fusion(f32[8,128]{1,0:T(8,128)S(1)} %get-tuple-element.5), kind=kLoop, calls=%fused_computation | loop fusion | bytes 24 | tf_op jit(solution)/shard_map/slice | solution.py:510
  56.0 0.7 %copy.10 = f32[114,4,128]{2,1,0:T(4,128)} copy(f32[114,4,128]{2,1,0:T(4,128)S(1)} %get-tuple-element.8) | data formatting | bytes 466944
Async XLA Ops:
  0.6 1.3 %copy-start = (bf16[1152,464]{1,0:T(8,128)(2,1)S(1)}, bf16[1152,464]{1,0:T(8,128)(2,1)}, u32[]{:S(2)}) copy-start(bf16[1152,464]{1,0:T(8,128)(2,1)} %constant.6.clone.low_hbm) | copy-start | bytes 3207172
  1.9 1.2 %copy-start.1 = (bf16[368,1152]{1,0:T(8,128)(2,1)S(1)}, bf16[368,1152]{1,0:T(8,128)(2,1)}, u32[]{:S(2)}) copy-start(bf16[368,1152]{1,0:T(8,128)(2,1)} %constant.7.clone.high_hbm) | copy-start | bytes 2543620
  3.1 1.0 %copy-start.2 = (f32[2,464,128]{2,1,0:T(8,128)S(1)}, f32[2,464,128]{2,1,0:T(8,128)}, u32[]{:S(2)}) copy-start(f32[2,464,128]{2,1,0:T(8,128)} %constant.8.clone.scale_ref) | copy-start | bytes 1425412
  4.1 0.9 %copy-start.3 = (f32[114,4,128]{2,1,0:T(4,128)S(1)}, f32[114,4,128]{2,1,0:T(4,128)}, u32[]{:S(2)}) copy-start(f32[114,4,128]{2,1,0:T(4,128)} %forcing_ref.1) | copy-start | bytes 700420
  5.0 0.7 %copy-start.4 = (f32[12,4,128]{2,1,0:T(4,128)S(1)}, f32[12,4,128]{2,1,0:T(4,128)}, u32[]{:S(2)}) copy-start(f32[12,4,128]{2,1,0:T(4,128)} %modes_ref.1) | copy-start | bytes 73732
  5.8 0.7 %copy-start.5 = (f32[4,128]{1,0:T(4,128)S(1)}, f32[4,128]{1,0:T(4,128)}, u32[]{:S(2)}) copy-start(f32[4,128]{1,0:T(4,128)} %mean_ref.1) | copy-start | bytes 6148
  6.4 0.7 %copy-start.6 = (s32[8]{0:T(128)S(1)}, s32[8]{0:T(128)}, u32[]{:S(2)}) copy-start(s32[8]{0:T(128)} %lengths_ref.1) | copy-start | bytes 100
where the time goes:
time: 57.1 us; the launch traced here: 56.7 us
  Pallas kernels  48.3 us (85%)
  local copies, waits for them, and re-layouts  7.77 us (14%)
  between operations  0.65 us (1%)
    pallas_call x1, Pallas kernels, local(): pl.pallas_call(functools.partial(kernel, groups, tiles, cap, rows, cols),...  48.3 us
    unnamed x15, local copies, waits for them, and re-layouts  7.14 us

commit v1 on v0

--- a/solution.py
+++ b/solution.py
@@ -63,10 +63,10 @@
     return hi, (x - hi.astype(F32)).astype(BF16)
 
 
-def kernel(groups, tiles, cap, rows, cols, lengths_ref, forcing_ref, mean_ref, modes_ref, low_hbm, high_hbm, scale_ref,
+def kernel(groups, tiles, cap, rows, cols, lengths_ref, forcing_hbm, mean_hbm, modes_hbm, low_hbm, high_hbm, scale_hbm,
            out_ref, norms_ref,
-           low_ref, high_ref, send_ref, recv_ref, own_ref, up_ref, down_ref, field_ref, coef_ref, dinv_ref,
-           hot_ref, d_ref, r_ref, s_ref, db_ref, v_ref, wb_ref, rsend_ref, rrecv_ref, part_ref, nbuf_ref, zpart_ref, zbuf_ref,
+           low_ref, high_ref, scale_ref, forcing_ref, send_ref, recv_ref, own_ref, to_up_ref, to_down_ref, up_ref, down_ref, field_ref, coef_ref, dinv_ref,
+           hot_ref, back_ref, d_ref, r_ref, s_ref, db_ref, v_ref, h_ref, wb_ref, rsend_ref, rrecv_ref, part_ref, nbuf_ref, zpart_ref, zbuf_ref,
            load_sem, f_send, f_recv, h_send, h_recv, a_send, a_recv, b_send, b_recv, n_send, n_recv, z_send, z_recv):
     me = lax.axis_index("chaos")
     sp = lax.axis_index("space")
@@ -79,10 +79,11 @@
     total_rows = rows + 2 * HALO
     mesh_id = pl.DeviceIdType.MESH
 
-    load_low = pltpu.make_async_copy(low_hbm, low_ref, load_sem.at[0])
-    load_high = pltpu.make_async_copy(high_hbm, high_ref, load_sem.at[1])
-    load_low.start()
-    load_high.start()
+    loads = [pltpu.make_async_copy(src, dst, load_sem.at[n]) for n, (src, dst) in enumerate((
+        (forcing_hbm, forcing_ref), (mean_hbm, field_ref.at[1, 0]), (modes_hbm, field_ref.at[1, 1:]),
+        (scale_hbm, scale_ref), (low_hbm, low_ref), (high_hbm, high_ref)))]
+    for load in loads:
+        load.start()
 
     barrier = pltpu.get_barrier_semaphore()
 
@@ -112,12 +113,6 @@
             send_ref[j, cap:capp, :] = jnp.zeros((capp - cap, 128), F32)
         return carry
 
-    lax.fori_loop(0, groups, pack, 0)
-    field_ref[1, 0] = mean_ref[...]
-    field_ref[1, 1:] = modes_ref[...]
-
-    pl.semaphore_wait(barrier, groups - 1 + tiles - 1)
-
     def a2a(j):
         c = lax.rem(me + j, groups)
         return pltpu.make_async_remote_copy(
@@ -134,7 +129,19 @@
         a2a(j).start()
         return carry
 
-    lax.fori_loop(1, groups, start_a2a, 0)
+    def pack_and_start(j, carry):
+        pack(j, carry)
+        a2a(j).start()
+        return carry
+
+    early = min(4, groups)
+    loads[0].wait()
+    for j in range(early):
+        pack(j, 0)
+    pl.semaphore_wait(barrier, groups - 1 + tiles - 1)
+    lax.fori_loop(1, early, start_a2a, 0)
+    loads[1].wait()
+    loads[2].wait()
 
     def column(src, dst, send, recv, target):
         return pltpu.make_async_remote_copy(
@@ -157,6 +164,7 @@
     def _():
         f_down.start()
 
+    lax.fori_loop(early, groups, pack_and_start, 0, unroll=groups <= 8)
     recv_ref[me] = send_ref[0]
 
     slots = groups * capp
@@ -173,6 +181,14 @@
     row = lax.broadcasted_iota(jnp.int32, (NP, slots), 0)
     row_coef = jnp.where(row < LOW, row, jnp.where(row < LP, -2, row - (LP - LOW)))
     hot_ref[...] = jnp.where(row_coef == coef, 1.0, 0.0).astype(BF16)
+    p_lane = lax.broadcasted_iota(jnp.int32, (half, NP), 1)
+    p_coef = jnp.where(p_lane < LOW, p_lane, jnp.where(p_lane < LP, -2, p_lane - (LP - LOW)))
+    t = lax.broadcasted_iota(jnp.int32, (half, NP), 0)
+    for h in range(2):
+        tt = t + h * half
+        for g in range(groups):
+            hot = jnp.where((tt < lengths_ref[g]) & (p_coef - tt == starts[g]), 1.0, 0.0).astype(BF16)
+            back_ref[h, g * half:(g + 1) * half, :] = hot
 
     @pl.when(jnp.logical_not(has_up))
     def _():
@@ -236,12 +252,35 @@
     lax.fori_loop(1, groups, wait_a2a, 0)
     hi, lo = halves(recv_ref[...].reshape(slots, 128))
     both = jnp.dot(hot_ref[...], jnp.concatenate([hi, lo], axis=1), preferred_element_type=F32)
-    own_ref[...] = (both[:, :128] + both[:, 128:]) * scale_ref[0]
-
-    h_up = column(own_ref, down_ref, h_send.at[0], h_recv.at[1], up_target)
-    h_down = column(own_ref, up_ref, h_send.at[1], h_recv.at[0], down_target)
-    h_from_up = column(own_ref, up_ref, h_send.at[0], h_recv.at[0], up_target)
-    h_from_down = column(own_ref, down_ref, h_send.at[1], h_recv.at[1], down_target)
+    loads[3].wait()
+    own = (both[:, :128] + both[:, 128:]) * scale_ref[0]
+    own_ref[...] = own
+
+    np2 = NP // 2
+    lane_2 = lax.broadcasted_iota(jnp.int32, (np2, 128), 1)
+    segments = []
+    offset = 0
+    for e in range(1, HALO + 1):
+        segments.append((e, offset, width + 2 * (HALO - e), SIDE - (HALO - e)))
+        offset += width + 2 * (HALO - e)
+
+    def pack_halo(row_at):
+        block = jnp.zeros((np2, 128), F32)
+        for part in range(2):
+            source = own[part * np2:(part + 1) * np2]
+            for e, offset, size, column_at in segments:
+                target = part * 64 + offset
+                rolled = pltpu.roll(source, (target - row_at(e) * stride - column_at) % 128, 1)
+                block = jnp.where((lane_2 >= target) & (lane_2 < target + size), rolled, block)
+        return block
+
+    to_up_ref[...] = pack_halo(lambda e: e - 1)
+    to_down_ref[...] = pack_halo(lambda e: rows - e)
+
+    h_up = column(to_up_ref, down_ref, h_send.at[0], h_recv.at[1], up_target)
+    h_down = column(to_down_ref, up_ref, h_send.at[1], h_recv.at[0], down_target)
+    h_from_up = column(to_down_ref, up_ref, h_send.at[0], h_recv.at[0], up_target)
+    h_from_down = column(to_up_ref, down_ref, h_send.at[1], h_recv.at[1], down_target)
 
     @pl.when(has_up)
     def _():
@@ -263,24 +302,36 @@
 
     lane_n = lax.broadcasted_iota(jnp.int32, (NP, 128), 1)
 
-    def spread(block, lower, upper, shift):
-        block = jnp.where((lane_n >= lower) & (lane_n < upper), block, 0.0)
-        if lanes > 128:
-            block = jnp.concatenate([block, jnp.zeros((NP, lanes - 128), F32)], axis=1)
-        return pltpu.roll(block, shift % lanes, 1)
-
-    above = (rows - HALO) * stride
-    r0 = spread(own_ref[...], 0, rows * stride, HALO * stride)
-    r0 = r0 + spread(up_ref[...], above, rows * stride, -above)
-    r0 = r0 + spread(down_ref[...], 0, HALO * stride, (HALO + rows) * stride)
-    r_ref[...] = r0
+    lane_w = lax.broadcasted_iota(jnp.int32, (np2, lanes), 1)
+
+    def wide(block, shift):
+        block = pltpu.roll(block, shift % 128, 1)
+        return jnp.concatenate([block] * (lanes // 128), axis=1) if lanes > 128 else block
+
+    def assemble(part):
+        mine = wide(own_ref[part * np2:(part + 1) * np2, :], HALO * stride)
+        block = jnp.where((lane_w >= HALO * stride) & (lane_w < (HALO + rows) * stride), mine, 0.0)
+        for source, row_at in ((up_ref[...], lambda e: HALO - e), (down_ref[...], lambda e: HALO + rows - 1 + e)):
+            for e, offset, size, column_at in segments:
+                target = row_at(e) * stride + column_at
+                moved = wide(source, target - part * 64 - offset)
+                block = jnp.where((lane_w >= target) & (lane_w < target + size), moved, block)
+        return block
 
     theta = (spectrum_high + spectrum_low) / 2.0
     delta = (spectrum_high - spectrum_low) / 2.0
     sigma = theta / delta
     rho = 1.0 / sigma
-    d_ref[...] = r0 * (dinv_ref[...] * (1.0 / theta))
-    s_ref[...] = d_ref[...]
+    for part in range(2):
+        here = slice(part * np2, (part + 1) * np2)
+        first = assemble(part)
+        r_ref[here, :] = first
+        first = first * (dinv_ref[...] * (1.0 / theta))
+        d_ref[here, :] = first
+        s_ref[here, :] = first
+        hi, lo = halves(first)
+        db_ref[here, 0:lanes] = hi
+        db_ref[here, lanes:] = lo
 
     own_lane = jnp.zeros((1, lanes), jnp.bool_)
     for r in range(rows):
@@ -288,8 +339,8 @@
         own_lane = own_lane | ((at >= 0) & (at < width))
     own_f = jnp.where(own_lane, 1.0, 0.0)
 
-    load_low.wait()
-    load_high.wait()
+    loads[4].wait()
+    loads[5].wait()
     part_ref[...] = jnp.zeros(part_ref.shape, F32)
 
     def neighbours(x):
@@ -298,50 +349,51 @@
 
     CH = 16
 
-    def split_rows(i, carry):
-        at = pl.multiple_of(i * CH, CH)
-        hi, lo = halves(d_ref[pl.ds(at, CH), :])
-        db_ref[pl.ds(at, CH), 0:lanes] = hi
-        db_ref[pl.ds(at, CH), lanes:] = lo
-        return carry
-
-    def low_terms(i, carry):
-        at = pl.multiple_of(i * CH, CH)
-        x = d_ref[pl.ds(at, CH), :]
+    def low_terms(at):
+        x = d_ref[at:at + CH, :]
         diffs = [x - y for y in neighbours(x)]
         for k in range(M):
             w = coef_ref[0, k + 1:k + 2, :] * diffs[0]
             for n in range(1, 4):
                 w = w + coef_ref[n, k + 1:k + 2, :] * diffs[n]
             hi, lo = halves(w)
-            there = pl.multiple_of(k * LP + at, CH)
-            wb_ref[pl.ds(there, CH), 0:lanes] = hi
-            wb_ref[pl.ds(there, CH), lanes:] = lo
-        return carry
-
-    def low_result(i, carry):
-        at = pl.multiple_of(i * CH, CH)
-        x = d_ref[pl.ds(at, CH), :]
+            wb_ref[k * LP + at:k * LP + at + CH, 0:lanes] = hi
+            wb_ref[k * LP + at:k * LP + at + CH, lanes:] = lo
+
+    def low_result(at):
+        x = d_ref[at:at + CH, :]
         sums = [coef_ref[n, 0:1, :] * x for n in range(4)]
         for k in range(M):
-            there = pl.multiple_of(k * LP + at, CH)
-            v = v_ref[pl.ds(there, CH), 0:lanes] + v_ref[pl.ds(there, CH), lanes:]
+            there = k * LP + at
+            v = v_ref[there:there + CH, 0:lanes] + v_ref[there:there + CH, lanes:]
             for n in range(4):
                 sums[n] = sums[n] + coef_ref[n, k + 1:k + 2, :] * v
         result = (sums[0] + sums[1]) + (sums[2] + sums[3])
         result = result - pltpu.roll(sums[0], 1, 1) - pltpu.roll(sums[1], lanes - 1, 1)
-        result = result - pltpu.roll(sums[2], stride, 1) - pltpu.roll(sums[3], lanes - stride, 1)
-        r_ref[pl.ds(at, CH), :] = r_ref[pl.ds(at, CH), :] - result
-        return carry
-
-    def high_result(i, carry):
-        at = pl.multiple_of(i * CH, CH)
-        x = d_ref[pl.ds(LP + at, CH), :]
-        result = v_ref[pl.ds(at, CH), 0:lanes] + v_ref[pl.ds(at, CH), lanes:]
+        return x, result - pltpu.roll(sums[2], stride, 1) - pltpu.roll(sums[3], lanes - stride, 1)
+
+    def high_result(at):
+        x = d_ref[LP + at:LP + at + CH, :]
+        result = h_ref[at:at + CH, 0:lanes] + h_ref[at:at + CH, lanes:]
         for n, y in enumerate(neighbours(x)):
             result = result + coef_ref[n, 0:1, :] * (x - y)
-        r_ref[pl.ds(LP + at, CH), :] = r_ref[pl.ds(LP + at, CH), :] - result
-        return carry
+        return x, result
+
+    def finish(at, x, result, factors):
+        residual = r_ref[at:at + CH, :] - result
+        scale = scale_ref[1, at:at + CH, :]
+        if lanes > 128:
+            scale = jnp.concatenate([scale] * (lanes // 128), axis=1)
+        scaled = residual * scale
+        if factors is not None:
+            r_ref[at:at + CH, :] = residual
+            new = factors[0] * x + factors[1] * (residual * dinv_ref[...])
+            d_ref[at:at + CH, :] = new
+            s_ref[at:at + CH, :] = s_ref[at:at + CH, :] + new
+            hi, lo = halves(new)
+            db_ref[at:at + CH, 0:lanes] = hi
+            db_ref[at:at + CH, lanes:] = lo
+        return scaled * scaled
 
     def back(j):
         c = lax.rem(me + j, groups)
@@ -366,21 +418,12 @@
             b = pltpu.roll(s, (piece + r * width - origin) % lanes, 1)[:, :128]
             q1 = jnp.where((lane_n >= r * width) & (lane_n < (r + 1) * width), a, q1)
             q2 = jnp.where((lane_n >= piece + r * width) & (lane_n < piece + (r + 1) * width), b, q2)
-        p_lane = lax.broadcasted_iota(jnp.int32, (half, NP), 1)
-        p_coef = jnp.where(p_lane < LOW, p_lane, jnp.where(p_lane < LP, -2, p_lane - (LP - LOW)))
-        t = lax.broadcasted_iota(jnp.int32, (half, NP), 0)
-        operands = []
-        for q in (q1, q2):
+        block = None
+        for h, q in enumerate((q1, q2)):
             hi, lo = halves(q * scale_ref[1])
-            operands.append(jnp.concatenate([hi, lo], axis=1))
-        for g in range(groups):
-            block = None
-            for h in range(2):
-                tt = t + h * half
-                hot = jnp.where((tt < lengths_ref[g]) & (p_coef == starts[g] + tt), 1.0, 0.0).astype(BF16)
-                term = jnp.dot(hot, operands[h], preferred_element_type=F32)
-                block = term if block is None else block + term
-            rsend_ref[g] = block[:, :128] + block[:, 128:]
+            term = jnp.dot(back_ref[h], jnp.concatenate([hi, lo], axis=1), preferred_element_type=F32)
+            block = term if block is None else block + term
+        rsend_ref[...] = (block[:, :128] + block[:, 128:]).reshape(groups, half, 128)
 
         def start_back(j, carry):
             back(j).start()
@@ -389,30 +432,28 @@
         lax.fori_loop(1, groups, start_back, 0)
         rrecv_ref[me] = rsend_ref[me]
 
-    weight = scale_ref[1] * scale_ref[1]
-    if lanes > 128:
-        weight = jnp.concatenate([weight] * (lanes // 128), axis=1)
     for step in range(ITERS):
-        lax.fori_loop(0, NP // CH, split_rows, 0)
-        lax.fori_loop(0, LP // CH, low_terms, 0)
         v_ref[...] = jnp.dot(low_ref[...], db_ref[...], preferred_element_type=F32)
-        lax.fori_loop(0, LP // CH, low_result, 0)
-        v_ref[0:HP, :] = jnp.dot(high_ref[...], wb_ref[...], preferred_element_type=F32)
-        lax.fori_loop(0, HP // CH, high_result, 0)
-        res = r_ref[...]
-        part = jnp.sum(res * res * weight, axis=0, keepdims=True) * own_f
+        for at in range(0, LP, CH):
+            low_terms(at)
+        h_ref[...] = jnp.dot(high_ref[...], wb_ref[...], preferred_element_type=F32)
+        factors = None
+        if step + 1 < ITERS:
+            rho_new = 1.0 / (2.0 * sigma - rho)
+            factors = (rho_new * rho, 2.0 * rho_new / delta)
+            rho = rho_new
+        squares = jnp.zeros((CH, lanes), F32)
+        for at in range(0, LP, CH):
+            squares = squares + finish(at, *low_result(at), factors)
+        for at in range(0, HP, CH):
+            squares = squares + finish(LP + at, *high_result(at), factors)
+        part = jnp.sum(squares, axis=0, keepdims=True) * own_f
         folded = part[:, 0:128]
         for extra in range(1, lanes // 128):
             folded = folded + part[:, extra * 128:(extra + 1) * 128]
         part_ref[step:step + 1, :] = folded
-        if step + 1 < ITERS:
-            rho_new = 1.0 / (2.0 * sigma - rho)
-            new = (rho_new * rho) * d_ref[...] + (2.0 * rho_new / delta) * (res * dinv_ref[...])
-            d_ref[...] = new
-            s_ref[...] = s_ref[...] + new
-            rho = rho_new
-            if step + 2 == ITERS:
-                send_back()
+        if step + 2 == ITERS:
+            send_back()
 
     def norm_copy(j, slot):
         c = lax.rem(me + j, groups)
@@ -482,29 +523,31 @@
     half = round_up(-(-cap // 2), 16)
     low, high, scales = tables()
     vmem = pl.BlockSpec(memory_space=pltpu.VMEM)
-    hbm = pl.BlockSpec(memory_space=pl.ANY)
+    hbm = pl.BlockSpec(memory_space=pltpu.HBM)
     dma = pltpu.SemaphoreType.DMA
     out, norms = pl.pallas_call(
         functools.partial(kernel, groups, tiles, cap, rows, cols),
         out_shape=(jax.ShapeDtypeStruct((cap, rows, cols), F32), jax.ShapeDtypeStruct((8, 128), F32)),
-        in_specs=[pl.BlockSpec(memory_space=pltpu.SMEM), vmem, vmem, vmem, hbm, hbm, vmem],
+        in_specs=[pl.BlockSpec(memory_space=pltpu.SMEM)] + [hbm] * 6,
         out_specs=(vmem, vmem),
         scratch_shapes=[
             pltpu.VMEM((M * LP, NP), BF16), pltpu.VMEM((HP, M * LP), BF16),
+            pltpu.VMEM((2, NP, 128), F32), pltpu.VMEM((cap, rows, cols), F32),
             pltpu.VMEM((groups, capp, 128), F32), pltpu.VMEM((groups, capp, 128), F32),
-            pltpu.VMEM((NP, 128), F32), pltpu.VMEM((NP, 128), F32), pltpu.VMEM((NP, 128), F32),
+            pltpu.VMEM((NP, 128), F32), *[pltpu.VMEM((NP // 2, 128), F32) for _ in range(4)],
             pltpu.VMEM((3, M + 1, rows, cols), F32), pltpu.VMEM((4, M + 1, lanes), F32), pltpu.VMEM((1, lanes), F32),
-            pltpu.VMEM((NP, groups * capp), BF16),
+            pltpu.VMEM((NP, groups * capp), BF16), pltpu.VMEM((2, groups * half, NP), BF16),
             pltpu.VMEM((NP, lanes), F32), pltpu.VMEM((NP, lanes), F32), pltpu.VMEM((NP, lanes), F32),
-            pltpu.VMEM((NP, 2 * lanes), BF16), pltpu.VMEM((M * LP, 2 * lanes), F32), pltpu.VMEM((M * LP, 2 * lanes), BF16),
+            pltpu.VMEM((NP, 2 * lanes), BF16), pltpu.VMEM((M * LP, 2 * lanes), F32), pltpu.VMEM((HP, 2 * lanes), F32),
+            pltpu.VMEM((M * LP, 2 * lanes), BF16),
             pltpu.VMEM((groups, half, 128), F32), pltpu.VMEM((groups, half, 128), F32),
             pltpu.VMEM((8, 128), F32), pltpu.VMEM((groups, 8, 128), F32),
             pltpu.VMEM((8, 128), F32), pltpu.VMEM((tiles, 8, 128), F32),
-            dma((2,)), dma((2,)), dma((2,)), dma((2,)), dma((2,)),
+            dma((6,)), dma((2,)), dma((2,)), dma((2,)), dma((2,)),
             dma((groups,)), dma((groups,)), dma((groups,)), dma((groups,)),
             dma((groups,)), dma((groups,)), dma((tiles,)), dma((tiles,)),
         ],
-        compiler_params=pltpu.CompilerParams(collective_id=0, has_side_effects=True, vmem_limit_bytes=48 * 2**20),
+        compiler_params=pltpu.CompilerParams(collective_id=0, has_side_effects=True, vmem_limit_bytes=60 * 2**20),
         name="chebyshev",
     )(lengths, forcing, mean_field, modes, jnp.asarray(low, BF16), jnp.asarray(high, BF16), jnp.asarray(scales))
     return out, norms[:ITERS, 0]

time: 57.1 us -> 38.6 us (0.68)
  Pallas kernels: 48.3 us -> 34.8 us
  local copies, waits for them, and re-layouts: 7.77 us -> 2.95 us
    pallas_call x1, Pallas kernels: 48.3 us -> 34.8 us  [local(): pl.pallas_call(functools.partial(kernel, groups, tiles, cap, rows, cols),...]
    unnamed x15 -> x1, local copies, waits for them, and re-layouts: 7.14 us -> 1.64 us
    slice x1, local copies, waits for them, and re-layouts: 0.63 us -> 1.31 us  [local(): return (out, norms[:ITERS, 0])]
where the time goes in v1:
time: 38.6 us; the launch traced here: 38.4 us
  Pallas kernels  34.8 us (90%)
  local copies, waits for them, and re-layouts  2.95 us (8%)
  between operations  0.64 us (2%)
    pallas_call x1, Pallas kernels, local(): pl.pallas_call(functools.partial(kernel, groups, tiles, cap, rows, cols),...  34.8 us
    unnamed x1, local copies, waits for them, and re-layouts  1.64 us
    slice x1, local copies, waits for them, and re-layouts, local(): return (out, norms[:ITERS, 0])  1.31 us

profile of v1, /device:TPU:0, one launch (start us, length us, event | category | flops | bytes accessed | tf_op | source)
XLA Modules:
  0.0 38.4 jit_solution(17793534587415620551)
XLA Ops:
  0.6 34.8 %chebyshev.1 = (f32[114,4,128]{2,1,0:T(4,128)}, f32[8,128]{1,0:T(8,128)}) custom-call(s32[8]{0:T(128)} %lengths_ref.1, f32[114,4,128]{2,1,0:T(4,128)} %forcing_hbm.1, f32[4,128]{1,0:T(4,128)} %mean_hbm.1, f32[12,4,128]{2,1,0:T(4,128)} %modes_hbm.1, bf16[1152,464]{1,0:T(8,128)(2,1)} %constant.6.clone.low_hbm, bf16[368,1152]{1,0:T(8,128)(2,1)} %constant.7.clone.high_hbm, ...), custom_call_target="tpu_custom_call" | custom-call | tf_op jit(solution)/shard_map/chebyshev/pallas_call | solution.py:528
  35.4 1.3 %slice_reduce_fusion = f32[3]{0:T(128)} fusion(f32[8,128]{1,0:T(8,128)} %get-tuple-element.5), kind=kLoop, calls=%fused_computation | loop fusion | bytes 24 | tf_op jit(solution)/shard_map/slice | solution.py:553
  36.7 1.6 %copy.10 = f32[114,4,128]{2,1,0:T(4,128)} copy(f32[114,4,128]{2,1,0:T(4,128)} %get-tuple-element.8) | data formatting | bytes 466944

commit v2 on v1

--- a/solution.py
+++ b/solution.py
@@ -490,17 +490,10 @@
         back_in(j).wait_recv()
         return carry
 
-    lax.fori_loop(1, groups, n_start, 0)
-    nbuf_ref[me] = part_ref[...]
-    lax.fori_loop(1, groups, n_wait, 0)
-    zpart_ref[...] = jnp.sum(nbuf_ref[...], axis=0)
-    lax.fori_loop(1, tiles, z_start, 0)
-    zbuf_ref[sp] = zpart_ref[...]
-
-    lax.fori_loop(1, groups, back_wait, 0)
     piece = rows * width
     lane_h = lax.broadcasted_iota(jnp.int32, (half, 128), 1)
-    for h in range(2):
+
+    def unpack(h):
         count = min(half, cap - h * half)
         for r in range(rows):
             block = jnp.zeros((half, 128), F32)
@@ -509,6 +502,15 @@
                 block = jnp.where((lane_h >= c * width) & (lane_h < (c + 1) * width), rolled, block)
             out_ref[h * half:h * half + count, r, :] = block[0:count]
 
+    lax.fori_loop(1, groups, n_start, 0)
+    nbuf_ref[me] = part_ref[...]
+    lax.fori_loop(1, groups, back_wait, 0)
+    unpack(0)
+    lax.fori_loop(1, groups, n_wait, 0)
+    zpart_ref[...] = jnp.sum(nbuf_ref[...], axis=0)
+    lax.fori_loop(1, tiles, z_start, 0)
+    zbuf_ref[sp] = zpart_ref[...]
+    unpack(1)
     lax.fori_loop(1, tiles, z_wait, 0)
     total = jnp.sum(jnp.sum(zbuf_ref[...], axis=0), axis=1, keepdims=True)
     norms_ref[...] = jnp.broadcast_to(jnp.sqrt(total), norms_ref.shape)

time: 38.6 us -> 38.6 us (level)
  no operation moved by 1% of the time
where the time goes in v2:
time: 38.6 us; the launch traced here: 38.4 us
  Pallas kernels  34.8 us (90%)
  local copies, waits for them, and re-layouts  2.95 us (8%)
  between operations  0.64 us (2%)
    pallas_call x1, Pallas kernels, local(): pl.pallas_call(functools.partial(kernel, groups, tiles, cap, rows, cols),...  34.8 us
    unnamed x1, local copies, waits for them, and re-layouts  1.64 us
    slice x1, local copies, waits for them, and re-layouts, local(): return (out, norms[:ITERS, 0])  1.31 us

profile of v2, /device:TPU:0, one launch (start us, length us, event | category | flops | bytes accessed | tf_op | source)
XLA Modules:
  0.0 38.4 jit_solution(11014101712906881490)
XLA Ops:
  0.6 34.8 %chebyshev.1 = (f32[114,4,128]{2,1,0:T(4,128)}, f32[8,128]{1,0:T(8,128)}) custom-call(s32[8]{0:T(128)} %lengths_ref.1, f32[114,4,128]{2,1,0:T(4,128)} %forcing_hbm.1, f32[4,128]{1,0:T(4,128)} %mean_hbm.1, f32[12,4,128]{2,1,0:T(4,128)} %modes_hbm.1, bf16[1152,464]{1,0:T(8,128)(2,1)} %constant.6.clone.low_hbm, bf16[368,1152]{1,0:T(8,128)(2,1)} %constant.7.clone.high_hbm, ...), custom_call_target="tpu_custom_call" | custom-call | tf_op jit(solution)/shard_map/chebyshev/pallas_call | solution.py:530
  35.4 1.3 %slice_reduce_fusion = f32[3]{0:T(128)} fusion(f32[8,128]{1,0:T(8,128)} %get-tuple-element.5), kind=kLoop, calls=%fused_computation | loop fusion | bytes 24 | tf_op jit(solution)/shard_map/slice | solution.py:555
  36.7 1.6 %copy.10 = f32[114,4,128]{2,1,0:T(4,128)} copy(f32[114,4,128]{2,1,0:T(4,128)} %get-tuple-element.8) | data formatting | bytes 466944
